TPU v7x, 128 devices: a whole 4x4x4 slice. The times are simulated.
128 devices in a mesh: fsdp: 128 (over z, y, x, core).
Axes of the slice: x: 4, y: 4, z: 4, core: 2. Of those that a mesh axis runs over, the one named last changes fastest.
Arguments:
- images: bfloat16 [384, 197, 768], P('fsdp'), may hold values from -6 to 6
- counts: int32 [128], P('fsdp'), may hold values from 2 to 3, as said below
- ln1_gain: bfloat16 [768], P('fsdp'), may hold values from 0.5 to 1.5
- ln1_bias: bfloat16 [768], P('fsdp'), may hold values from -1.1953125 to 1.1953125
- qkv_weight: bfloat16 [768, 2304], P('fsdp'), may hold values from -0.21875 to 0.21875
- qkv_bias: bfloat16 [1536], P('fsdp'), may hold values from -1.1953125 to 1.1953125
- out_weight: bfloat16 [768, 768], P('fsdp'), may hold values from -0.625 to 0.625
- out_bias: bfloat16 [768], P('fsdp'), may hold values from -1.1953125 to 1.1953125
- ln2_gain: bfloat16 [768], P('fsdp'), may hold values from 0.5 to 1.5
- ln2_bias: bfloat16 [768], P('fsdp'), may hold values from -1.1953125 to 1.1953125
- fc1_weight: bfloat16 [768, 3072], P('fsdp'), may hold values from -0.21875 to 0.21875
- fc1_bias: bfloat16 [3072], P('fsdp'), may hold values from -1.1953125 to 1.1953125
- fc2_weight: bfloat16 [3072, 768], P('fsdp'), may hold values from -0.109375 to 0.109375
- fc2_bias: bfloat16 [768], P('fsdp'), may hold values from -1.1953125 to 1.1953125
- d_out: bfloat16 [384, 197, 768], P('fsdp'), may hold values from -6 to 6
Outputs:
- out_images: bfloat16 [384, 197, 768], P('fsdp')
- d_images: bfloat16 [384, 197, 768], P('fsdp')
- d_ln1_gain: float32 [768], P('fsdp')
- d_ln1_bias: float32 [768], P('fsdp')
- d_qkv_weight: float32 [768, 2304], P('fsdp')
- d_qkv_bias: float32 [1536], P('fsdp')
- d_out_weight: float32 [768, 768], P('fsdp')
- d_out_bias: float32 [768], P('fsdp')
- d_ln2_gain: float32 [768], P('fsdp')
- d_ln2_bias: float32 [768], P('fsdp')
- d_fc1_weight: float32 [768, 3072], P('fsdp')
- d_fc1_bias: float32 [3072], P('fsdp')
- d_fc2_weight: float32 [3072, 768], P('fsdp')
- d_fc2_bias: float32 [768], P('fsdp')
Inputs may be any that keep to these rules, and one draw needn't show every extreme that they name: `counts`: each device holds 2 or 3 images in its first slots; some device holds each of the two numbers.
All inputs are finite; a program needn't handle non-finite values.
Results may differ from a plain program's by a relative error of at most 0.019.
Values may be sent and summed in bfloat16 or wider, within the bound.
No kernel may reach another device: no remote copies, remote signals or barrier semaphores. Data moves between devices by JAX's collectives and lax.ppermute only.
A program may use at most 192 MiB of HBM per device.

v0:
```python
import math

import jax
import jax.numpy as jnp
from jax import lax
from jax.sharding import PartitionSpec as P

H = 12
HD = 64


eps_norm = 1e-06


def normalize(values, gain_vec, offset):
    average = jnp.mean(values, -1, keepdims=True)
    centered = values - average
    spread = jnp.mean(centered * centered, -1, keepdims=True)
    return centered * lax.rsqrt(spread + eps_norm) * gain_vec + offset


def exact_gelu(values):
    return jax.nn.gelu(values, approximate=False)


def mat_product(left, right):
    return jnp.dot(left, right, preferred_element_type=jnp.float32)


def grad_weight(left, right):
    return jnp.einsum("ra,rb->ab", left, right, preferred_element_type=jnp.float32)


def grad_input(grad_low, matrix):
    return jnp.einsum("rb,ab->ra", grad_low, matrix, preferred_element_type=jnp.float32)


def column_sums(grad_low):
    return jnp.sum(grad_low, axis=0, dtype=jnp.float32)


def local(
    images,
    counts,
    ln1_gain,
    ln1_bias,
    qkv_weight,
    qkv_bias,
    out_weight,
    out_bias,
    ln2_gain,
    ln2_bias,
    fc1_weight,
    fc1_bias,
    fc2_weight,
    fc2_bias,
    d_out,
):
    slot_count, seq_len, feature_width = images.shape
    row_count = slot_count * seq_len
    score_scale = 1.0 / math.sqrt(HD)
    attn_local = (ln1_gain, ln1_bias, qkv_weight, qkv_bias, out_weight, out_bias)
    mlp_local = (ln2_gain, ln2_bias, fc1_weight, fc1_bias, fc2_weight, fc2_bias)
    attn_full = (
        lax.all_gather(attn_local[0], "fsdp", axis=0, tiled=True),
        lax.all_gather(attn_local[1], "fsdp", axis=0, tiled=True),
        lax.all_gather(attn_local[2], "fsdp", axis=0, tiled=True),
        lax.all_gather(attn_local[3], "fsdp", axis=0, tiled=True),
        lax.all_gather(attn_local[4], "fsdp", axis=0, tiled=True),
        lax.all_gather(attn_local[5], "fsdp", axis=0, tiled=True),
    )
    gain_one, offset_one, qkv_matrix, qkv_offset, out_matrix, out_offset = attn_full
    gain_one = gain_one.astype(jnp.float32)
    offset_one = offset_one.astype(jnp.float32)
    slot_live = (jnp.arange(slot_count, dtype=jnp.int32) < counts[0]).astype(jnp.float32)
    row_live = jnp.repeat(slot_live, seq_len)[:, None]
    inputs = images.reshape(row_count, feature_width).astype(jnp.float32)
    normed_one = normalize(inputs, gain_one, offset_one).astype(jnp.bfloat16)
    bias_full = jnp.concatenate(
        [
            qkv_offset[:feature_width].astype(jnp.float32),
            jnp.zeros((feature_width,), jnp.float32),
            qkv_offset[feature_width:].astype(jnp.float32),
        ]
    )
    project = (mat_product(normed_one, qkv_matrix) + bias_full).astype(jnp.bfloat16)
    queries = project[:, :feature_width].reshape(slot_count, seq_len, H, HD)
    key_heads = project[:, feature_width : 2 * feature_width].reshape(slot_count, seq_len, H, HD)
    value_heads = project[:, 2 * feature_width :].reshape(slot_count, seq_len, H, HD)
    scores = (
        jnp.einsum("gqhd,gkhd->ghqk", queries, key_heads, preferred_element_type=jnp.float32)
        * score_scale
    )
    log_total = jax.nn.logsumexp(scores, axis=-1, keepdims=True)
    probs_low = jnp.exp(scores - log_total).astype(jnp.bfloat16)
    mixed_heads = jnp.einsum(
        "ghqk,gkhd->gqhd", probs_low, value_heads, preferred_element_type=jnp.float32
    )
    mixed_low = mixed_heads.reshape(row_count, feature_width).astype(jnp.bfloat16)
    after_attn = inputs + mat_product(mixed_low, out_matrix) + out_offset.astype(jnp.float32)
    mlp_full = (
        lax.all_gather(mlp_local[0], "fsdp", axis=0, tiled=True),
        lax.all_gather(mlp_local[1], "fsdp", axis=0, tiled=True),
        lax.all_gather(mlp_local[2], "fsdp", axis=0, tiled=True),
        lax.all_gather(mlp_local[3], "fsdp", axis=0, tiled=True),
        lax.all_gather(mlp_local[4], "fsdp", axis=0, tiled=True),
        lax.all_gather(mlp_local[5], "fsdp", axis=0, tiled=True),
    )
    gain_two = mlp_full[0].astype(jnp.float32)
    offset_two = mlp_full[1].astype(jnp.float32)
    normed_two = normalize(after_attn, gain_two, offset_two).astype(jnp.bfloat16)
    pre_act = mat_product(normed_two, mlp_full[2]) + mlp_full[3].astype(jnp.float32)
    hidden, gelu_back = jax.vjp(exact_gelu, pre_act)
    hidden_low = hidden.astype(jnp.bfloat16)
    branch_two = mat_product(hidden_low, mlp_full[4]) + mlp_full[5].astype(jnp.float32)
    out_images = (
        ((after_attn + branch_two) * row_live)
        .reshape(slot_count, seq_len, feature_width)
        .astype(jnp.bfloat16)
    )
    mlp_back = (
        lax.all_gather(mlp_local[0], "fsdp", axis=0, tiled=True),
        lax.all_gather(mlp_local[1], "fsdp", axis=0, tiled=True),
        lax.all_gather(mlp_local[2], "fsdp", axis=0, tiled=True),
        lax.all_gather(mlp_local[3], "fsdp", axis=0, tiled=True),
        lax.all_gather(mlp_local[4], "fsdp", axis=0, tiled=True),
        lax.all_gather(mlp_local[5], "fsdp", axis=0, tiled=True),
    )
    g_branch_f = d_out.reshape(row_count, feature_width).astype(jnp.float32) * row_live
    g_branch = g_branch_f.astype(jnp.bfloat16)
    d_fc2_bias = column_sums(g_branch)
    d_fc2_weight = grad_weight(hidden_low, g_branch)
    g_hidden = grad_input(g_branch, mlp_back[4])
    g_pre = gelu_back(g_hidden)[0].astype(jnp.bfloat16)
    d_fc1_bias = column_sums(g_pre)
    d_fc1_weight = grad_weight(normed_two, g_pre)
    g_normed_two = grad_input(g_pre, mlp_back[2])
    norm_two_back = jax.vjp(normalize, after_attn, gain_two, offset_two)[1]
    g_after_part, d_ln2_gain, d_ln2_bias = norm_two_back(g_normed_two)
    g_after = g_branch_f + g_after_part
    mlp_grads = (d_ln2_gain, d_ln2_bias, d_fc1_weight, d_fc1_bias, d_fc2_weight, d_fc2_bias)
    mlp_owned = (
        lax.psum_scatter(mlp_grads[0], "fsdp", scatter_dimension=0, tiled=True),
        lax.psum_scatter(mlp_grads[1], "fsdp", scatter_dimension=0, tiled=True),
        lax.psum_scatter(mlp_grads[2], "fsdp", scatter_dimension=0, tiled=True),
        lax.psum_scatter(mlp_grads[3], "fsdp", scatter_dimension=0, tiled=True),
        lax.psum_scatter(mlp_grads[4], "fsdp", scatter_dimension=0, tiled=True),
        lax.psum_scatter(mlp_grads[5], "fsdp", scatter_dimension=0, tiled=True),
    )
    attn_back = (
        lax.all_gather(attn_local[0], "fsdp", axis=0, tiled=True),
        lax.all_gather(attn_local[1], "fsdp", axis=0, tiled=True),
        lax.all_gather(attn_local[2], "fsdp", axis=0, tiled=True),
        lax.all_gather(attn_local[3], "fsdp", axis=0, tiled=True),
        lax.all_gather(attn_local[4], "fsdp", axis=0, tiled=True),
        lax.all_gather(attn_local[5], "fsdp", axis=0, tiled=True),
    )
    g_attn = g_after.astype(jnp.bfloat16)
    d_out_bias = column_sums(g_attn)
    d_out_weight = grad_weight(mixed_low, g_attn)
    g_mixed = (
        grad_input(g_attn, attn_back[4]).astype(jnp.bfloat16).reshape(slot_count, seq_len, H, HD)
    )
    scores_again = (
        jnp.einsum("gqhd,gkhd->ghqk", queries, key_heads, preferred_element_type=jnp.float32)
        * score_scale
    )
    probs_again = jnp.exp(scores_again - log_total)
    g_probs = jnp.einsum(
        "gqhd,gkhd->ghqk", g_mixed, value_heads, preferred_element_type=jnp.float32
    )
    g_values = jnp.einsum(
        "ghqk,gqhd->gkhd",
        probs_again.astype(jnp.bfloat16),
        g_mixed,
        preferred_element_type=jnp.float32,
    )
    row_delta = jnp.sum(g_probs * probs_again, axis=-1, keepdims=True)
    g_scores = (probs_again * (g_probs - row_delta)).astype(jnp.bfloat16)
    g_queries = (
        jnp.einsum("ghqk,gkhd->gqhd", g_scores, key_heads, preferred_element_type=jnp.float32)
        * score_scale
    )
    g_keys = (
        jnp.einsum("ghqk,gqhd->gkhd", g_scores, queries, preferred_element_type=jnp.float32)
        * score_scale
    )
    g_qkv = jnp.concatenate(
        [
            g_queries.reshape(row_count, feature_width),
            g_keys.reshape(row_count, feature_width),
            g_values.reshape(row_count, feature_width),
        ],
        axis=1,
    ).astype(jnp.bfloat16)
    qkv_sums = column_sums(g_qkv)
    d_qkv_bias = jnp.concatenate([qkv_sums[:feature_width], qkv_sums[2 * feature_width :]])
    d_qkv_weight = grad_weight(normed_one, g_qkv)
    g_normed_one = grad_input(g_qkv, attn_back[2])
    norm_one_back = jax.vjp(normalize, inputs, gain_one, offset_one)[1]
    g_input_part, d_ln1_gain, d_ln1_bias = norm_one_back(g_normed_one)
    d_images = (
        (g_after + g_input_part).reshape(slot_count, seq_len, feature_width).astype(jnp.bfloat16)
    )
    attn_grads = (d_ln1_gain, d_ln1_bias, d_qkv_weight, d_qkv_bias, d_out_weight, d_out_bias)
    attn_owned = (
        lax.psum_scatter(attn_grads[0], "fsdp", scatter_dimension=0, tiled=True),
        lax.psum_scatter(attn_grads[1], "fsdp", scatter_dimension=0, tiled=True),
        lax.psum_scatter(attn_grads[2], "fsdp", scatter_dimension=0, tiled=True),
        lax.psum_scatter(attn_grads[3], "fsdp", scatter_dimension=0, tiled=True),
        lax.psum_scatter(attn_grads[4], "fsdp", scatter_dimension=0, tiled=True),
        lax.psum_scatter(attn_grads[5], "fsdp", scatter_dimension=0, tiled=True),
    )
    return (
        out_images,
        d_images,
        attn_owned[0],
        attn_owned[1],
        attn_owned[2],
        attn_owned[3],
        attn_owned[4],
        attn_owned[5],
        mlp_owned[0],
        mlp_owned[1],
        mlp_owned[2],
        mlp_owned[3],
        mlp_owned[4],
        mlp_owned[5],
    )


def solution(mesh):
    in_specs = (
        P("fsdp", None, None),
        P("fsdp"),
        P("fsdp"),
        P("fsdp"),
        P("fsdp", None),
        P("fsdp"),
        P("fsdp", None),
        P("fsdp"),
        P("fsdp"),
        P("fsdp"),
        P("fsdp", None),
        P("fsdp"),
        P("fsdp", None),
        P("fsdp"),
        P("fsdp", None, None),
    )
    out_specs = (
        P("fsdp", None, None),
        P("fsdp", None, None),
        P("fsdp"),
        P("fsdp"),
        P("fsdp", None),
        P("fsdp"),
        P("fsdp", None),
        P("fsdp"),
        P("fsdp"),
        P("fsdp"),
        P("fsdp", None),
        P("fsdp"),
        P("fsdp", None),
        P("fsdp"),
    )
    return jax.shard_map(local, mesh=mesh, in_specs=in_specs, out_specs=out_specs, check_vma=False)
```

profile of v0, /device:TPU:1, one launch (start us, length us, event | category | flops | bytes accessed | tf_op | source)
XLA Modules:
  0.0 1197.8 jit_solution(7913958524995386396)
XLA Ops:
  15.4 69.5 %all-reduce.23 = (bf16[1536]{0:T(1024)(128)(2,1)S(1)}, bf16[768]{0:T(1024)(128)(2,1)S(1)}, bf16[768]{0:T(1024)(128)(2,1)S(1)}, bf16[768]{0:T(1024)(128)(2,1)S(1)...) all-reduce(bf16[1536]{0:T(1024)(128)(2,1)S(1)} %dynamic-update-slic, ...), channel_id=1, replica_groups=mesh['fsdp'=128] {'fsdp'}, use_global_device_ids=true, to_apply=%add.2 | all-reduce | flops 9216 | bytes 36864
  93.4 52.9 %all-gather.10.cloned.1.call-done = bf16[128,6,2304]{2,1,0:T(8,128)(2,1)} async-done(((bf16[1,6,2304]{2,1,0:T(8,128)(2,1)}), bf16[128,6,2304]{2,1,0:T(8,128)(2,1)}) %all-gather.10.cloned.1.call-update) | async-done | bytes 3538960 | tf_op jit(solution)/shard_map/all_gather | solution.py:67
  146.3 6.6 reshape.200
  153.0 4.4 add_convert_fusion.1
  173.0 3.5 copy.66
  187.9 27.3 %all-gather.14.cloned.1.call-done = bf16[128,6,3072]{2,1,0:T(8,128)(2,1)} async-done(((bf16[1,6,3072]{2,1,0:T(8,128)(2,1)}), bf16[128,6,3072]{2,1,0:T(8,128)(2,1)}) %all-gather.14.cloned.1.call-update) | async-done | bytes 4718608 | tf_op jit(solution)/shard_map/all_gather | solution.py:104
  215.2 7.7 reshape.204
  222.9 22.2 %multiply_convert_fusion.1 = (bf16[591,3072]{1,0:T(8,128)(2,1)}, f32[591,3072]{1,0:T(8,128)}, f32[591,3072]{1,0:T(8,128)}) fusion(f32[3072]{0:T(1024)S(1)} %copy-done.124, bf16[768,3072]{1,0:T(8,128)(2,1)} %reshape.204, f32[591,768]{1,0:T(8,128)S(1)} %get-tuple-element.60, f32[768]{0:T(1024)S(1)} %convert_element_type.133, ...), kind=kOutput, calls=%fused_computation.8 | convolution fusion | flops 2910783744 | bytes 24712824 | tf_op jit(solution)/shard_map/dot_general | solution.py:27
  245.1 37.7 %all-gather.8.cloned.1.call-done = bf16[3072,768]{1,0:T(8,128)(2,1)} async-done(((bf16[24,768]{1,0:T(8,128)(2,1)}), bf16[3072,768]{1,0:T(8,128)(2,1)}) %all-gather.8.cloned.1.call-update) | async-done | bytes 4718608 | tf_op jit(solution)/shard_map/all_gather | solution.py:106
  282.8 12.0 convert_reduce_fusion
  294.8 3.9 multiply_reduce_fusion.3
  301.9 6.4 fusion.22
  320.8 5.1 fusion.13
  328.1 4.2 reshape.180
  332.3 6.2 multiply_reduce_fusion
  358.7 5.8 fusion.24
  364.5 6.9 fusion.25
  371.4 365.5 %fusion.27 = (f32[8,2304]{1,0:T(8,128)S(1)}, f32[8,768]{1,0:T(8,128)S(1)}, f32[8,3072]{1,0:T(8,128)S(1)}) fusion(f32[768,2304]{1,0:T(8,128)} %fusion.24, f32[768,768]{1,0:T(8,128)} %fusion.17, f32[768,3072]{1,0:T(8,128)} %fusion.25), kind=kCustom, calls=%all-reduce-scatter.3 | all-reduce-scatter fusion | flops 6291457 | bytes 19070976
  750.7 14.0 %collective-permute-start.41 = (f32[8,768]{1,0:T(8,128)S(1)}, f32[8,768]{1,0:T(8,128)S(1)}, u32[]{:S(2)}, u32[]{:S(2)}) collective-permute-start(f32[8,768]{1,0:T(8,128)S(1)} %get-tuple-element.40), channel_id=1, source_target_pairs={{0,10},{1,11},{2,12},{3,13},{4,14},{5,15},{6,16},{7,17},{8,18},{9,... | collective-permute-start | bytes 73736
  769.0 5.8 collective-permute-start.44
  774.8 11.4 collective-permute-start.45
  786.2 3.8 collective-permute-start.46
  790.1 4.6 collective-permute-start.47
  813.6 3.5 collective-permute-start.58
  827.0 4.5 collective-permute-start.61
  835.7 4.7 collective-permute-start.10
  840.4 5.3 collective-permute-start.11
  845.7 5.8 collective-permute-start.12
  851.5 4.5 collective-permute-start.13
  856.1 4.0 collective-permute-start.14
  868.3 3.5 collective-permute-start.18
  874.7 7.9 multiply_convert_fusion.5
  901.4 3.8 collective-permute-start.27
  911.1 3.7 collective-permute-start.4
  924.0 4.5 collective-permute-start.7
  930.5 6.0 collective-permute-start.9
  937.9 4.3 collective-permute-start.66
  942.3 3.6 collective-permute-start.67
  946.0 4.0 collective-permute-start.68
  952.0 3.5 collective-permute-start.70
  985.4 7.3 collective-permute-start.84
  992.7 63.0 %all-reduce.22 = (f32[768]{0:T(1024)}, f32[768]{0:T(1024)}, f32[1536]{0:T(1024)}, f32[768]{0:T(1024)S(1)}, f32[768]{0:T(1024)S(1)}, /*index=5*/f32[768]{0:T(1024)S(1)}, f32[3072]{0:T(1024)}, f32[768]{0:T(1024)}) all-reduce(f32[768]{0:T(1024)S(1)} %copy-done.130, ...), channel_id=2, replica_groups=mesh['fsdp'=128] {'fsdp'}, use_global_device_ids=true, to_apply=%region_12.0.clone | all-reduce | flops 9216 | bytes 73728
  1066.1 26.4 %concatenate.14 = f32[262,768]{1,0:T(8,128)S(1)} concatenate(f32[6,768]{1,0:T(8,128)} %copy-done.90, f32[8,768]{1,0:T(8,128)} %copy-done.119, f32[8,768]{1,0:T(8,128)} %copy-done.118, f32[8,768]{1,0:T(8,128)} %copy-done.117, f32[8,768]{1,0:T(8,128)} %copy-done.116, f32[8,768]{1,0:T(8,128)} %copy-done.115, f32[8,768]{1,0:T(8,128)} %copy-done.114, f32[8,768]{1,0:T(8,128)} %copy-done.113, ...), dimensions={0} | concatenate | bytes 1609728
  1092.6 4.9 collective-permute-start.85
  1097.5 4.1 collective-permute-start.86
  1106.7 4.5 collective-permute-start.89
  1111.9 32.6 %concatenate.13 = f32[262,2304]{1,0:T(8,128)S(1)} concatenate(f32[6,2304]{1,0:T(8,128)} %copy-done.57, f32[8,2304]{1,0:T(8,128)} %copy-done.78, f32[8,2304]{1,0:T(8,128)} %copy-done.76, f32[8,2304]{1,0:T(8,128)} %copy-done.75, f32[8,2304]{1,0:T(8,128)} %copy-done.74, f32[8,2304]{1,0:T(8,128)} %copy-done.73, f32[8,2304]{1,0:T(8,128)} %copy-done.72, f32[8,2304]{1,0:T(8,128)} %copy-done.71, ...), dimensions={0} | concatenate | bytes 4829184
  1158.9 31.5 %concatenate.15 = f32[262,3072]{1,0:T(8,128)S(1)} concatenate(f32[6,3072]{1,0:T(8,128)S(1)} %collective-permute-done.95, f32[8,3072]{1,0:T(8,128)} %collective-permute-done.94, f32[8,3072]{1,0:T(8,128)} %copy-done.54, f32[8,3072]{1,0:T(8,128)} %copy-done.53, f32[8,3072]{1,0:T(8,128)} %copy-done.52, f32[8,3072]{1,0:T(8,128)} %copy-done.51, f32[8,3072]{1,0:T(8,128)} %copy-done.50, ...), dimensions={0} | concatenate | bytes 6438912
  (570 shorter events, 241.1 us)
Async XLA Ops:
  7.3 82.9 %all-gather.12.cloned.1.call-start = ((), (), s32[]{:S(2)}) async-start(), calls=%async_computation.4 | async-start | bytes 1585152 | tf_op jit(solution)/shard_map/all_gather | solution.py:69
  8.0 138.3 %all-gather.10.cloned.1.call-start = ((), (), s32[]{:S(2)}) async-start(), calls=%async_computation.3 | async-start | bytes 4755456 | tf_op jit(solution)/shard_map/all_gather | solution.py:67
  8.8 206.4 %all-gather.14.cloned.1.call-start = ((), (), s32[]{:S(2)}) async-start(), calls=%async_computation.5 | async-start | bytes 6340608 | tf_op jit(solution)/shard_map/all_gather | solution.py:104
  9.5 273.3 %all-gather.8.cloned.1.call-start = ((), (), s32[]{:S(2)}) async-start(), calls=%async_computation.1 | async-start | bytes 4755456 | tf_op jit(solution)/shard_map/all_gather | solution.py:106
  10.1 1181.0 %reduce-scatter.8.cloned.1.call-start = ((), (), s32[]{:S(2)}) async-start(), calls=%async_computation.2 | async-start | bytes 9510912 | tf_op jit(solution)/shard_map/reduce_scatter | solution.py:147
  745.3 19.5 %collective-permute-start.37 = (f32[8,768]{1,0:T(8,128)S(1)}, f32[8,768]{1,0:T(8,128)S(1)}, u32[]{:S(2)}, u32[]{:S(2)}) collective-permute-start(f32[8,768]{1,0:T(8,128)S(1)} %get-tuple-element.40), channel_id=1, source_target_pairs={{0,6},{1,7},{2,8},{3,9},{4,10},{5,11},{6,12},{7,13},{8,14},{9,15},... | collective-permute-start | bytes 73736
  746.6 21.0 %collective-permute-start.38 = (f32[8,768]{1,0:T(8,128)S(1)}, f32[8,768]{1,0:T(8,128)S(1)}, u32[]{:S(2)}, u32[]{:S(2)}) collective-permute-start(f32[8,768]{1,0:T(8,128)S(1)} %get-tuple-element.40), channel_id=1, source_target_pairs={{0,7},{1,8},{2,9},{3,10},{4,11},{5,12},{6,13},{7,14},{8,15},{9,16}... | collective-permute-start | bytes 73736
  747.9 21.1 %collective-permute-start.39 = (f32[8,768]{1,0:T(8,128)S(1)}, f32[8,768]{1,0:T(8,128)S(1)}, u32[]{:S(2)}, u32[]{:S(2)}) collective-permute-start(f32[8,768]{1,0:T(8,128)S(1)} %get-tuple-element.40), channel_id=1, source_target_pairs={{0,8},{1,9},{2,10},{3,11},{4,12},{5,13},{6,14},{7,15},{8,16},{9,17... | collective-permute-start | bytes 73736
  749.3 25.5 %collective-permute-start.40 = (f32[8,768]{1,0:T(8,128)S(1)}, f32[8,768]{1,0:T(8,128)S(1)}, u32[]{:S(2)}, u32[]{:S(2)}) collective-permute-start(f32[8,768]{1,0:T(8,128)S(1)} %get-tuple-element.40), channel_id=1, source_target_pairs={{0,9},{1,10},{2,11},{3,12},{4,13},{5,14},{6,15},{7,16},{8,17},{9,1... | collective-permute-start | bytes 73736
  750.7 35.5 %collective-permute-start.41 = (f32[8,768]{1,0:T(8,128)S(1)}, f32[8,768]{1,0:T(8,128)S(1)}, u32[]{:S(2)}, u32[]{:S(2)}) collective-permute-start(f32[8,768]{1,0:T(8,128)S(1)} %get-tuple-element.40), channel_id=1, source_target_pairs={{0,10},{1,11},{2,12},{3,13},{4,14},{5,15},{6,16},{7,17},{8,18},{9,... | collective-permute-start | bytes 73736
  764.8 25.3 %collective-permute-start.42 = (f32[8,768]{1,0:T(8,128)S(1)}, f32[8,768]{1,0:T(8,128)S(1)}, u32[]{:S(2)}, u32[]{:S(2)}) collective-permute-start(f32[8,768]{1,0:T(8,128)S(1)} %get-tuple-element.40), channel_id=1, source_target_pairs={{0,11},{1,12},{2,13},{3,14},{4,15},{5,16},{6,17},{7,18},{8,19},{9,... | collective-permute-start | bytes 73736
  767.6 27.0 %collective-permute-start.43 = (f32[8,768]{1,0:T(8,128)S(1)}, f32[8,768]{1,0:T(8,128)S(1)}, u32[]{:S(2)}, u32[]{:S(2)}) collective-permute-start(f32[8,768]{1,0:T(8,128)S(1)} %get-tuple-element.40), channel_id=1, source_target_pairs={{0,12},{1,13},{2,14},{3,15},{4,16},{5,17},{6,18},{7,19},{8,20},{9,... | collective-permute-start | bytes 73736
  769.0 27.5 %collective-permute-start.44 = (f32[8,768]{1,0:T(8,128)S(1)}, f32[8,768]{1,0:T(8,128)S(1)}, u32[]{:S(2)}, u32[]{:S(2)}) collective-permute-start(f32[8,768]{1,0:T(8,128)S(1)} %get-tuple-element.40), channel_id=1, source_target_pairs={{0,13},{1,14},{2,15},{3,16},{4,17},{5,18},{6,19},{7,20},{8,21},{9,... | collective-permute-start | bytes 73736
  774.8 23.4 %collective-permute-start.45 = (f32[8,768]{1,0:T(8,128)S(1)}, f32[8,768]{1,0:T(8,128)S(1)}, u32[]{:S(2)}, u32[]{:S(2)}) collective-permute-start(f32[8,768]{1,0:T(8,128)S(1)} %get-tuple-element.40), channel_id=1, source_target_pairs={{0,14},{1,15},{2,16},{3,17},{4,18},{5,19},{6,20},{7,21},{8,22},{9,... | collective-permute-start | bytes 73736
  786.2 15.4 %collective-permute-start.46 = (f32[8,768]{1,0:T(8,128)S(1)}, f32[8,768]{1,0:T(8,128)S(1)}, u32[]{:S(2)}, u32[]{:S(2)}) collective-permute-start(f32[8,768]{1,0:T(8,128)S(1)} %get-tuple-element.40), channel_id=1, source_target_pairs={{0,15},{1,16},{2,17},{3,18},{4,19},{5,20},{6,21},{7,22},{8,23},{9,... | collective-permute-start | bytes 73736
  820.1 25.5 %collective-permute-start.95 = (f32[6,3072]{1,0:T(8,128)S(1)}, f32[6,3072]{1,0:T(8,128)S(1)}, u32[]{:S(2)}, u32[]{:S(2)}) collective-permute-start(f32[6,3072]{1,0:T(8,128)S(1)} %slice.37), channel_id=1, source_target_pairs={{0,32},{1,33},{2,34},{3,35},{4,36},{5,37},{6,38},{7,39},{8,40},{9,... | collective-permute-start | bytes 221192
  821.5 30.0 %collective-permute-start = (f32[8,2304]{1,0:T(8,128)S(1)}, f32[8,2304]{1,0:T(8,128)S(1)}, u32[]{:S(2)}, u32[]{:S(2)}) collective-permute-start(f32[8,2304]{1,0:T(8,128)S(1)} %get-tuple-element.39), channel_id=1, source_target_pairs={{0,1},{1,2},{2,3},{3,4},{4,5},{5,6},{6,7},{7,8},{8,9},{9,10},{10,1... | collective-permute-start | bytes 221192
  823.7 32.3 %collective-permute-start.1 = (f32[8,2304]{1,0:T(8,128)S(1)}, f32[8,2304]{1,0:T(8,128)S(1)}, u32[]{:S(2)}, u32[]{:S(2)}) collective-permute-start(f32[8,2304]{1,0:T(8,128)S(1)} %get-tuple-element.39), channel_id=1, source_target_pairs={{0,2},{1,3},{2,4},{3,5},{4,6},{5,7},{6,8},{7,9},{8,10},{9,11},{10,... | collective-permute-start | bytes 221192
  825.5 14.9 %collective-permute-start.31 = (f32[6,2304]{1,0:T(8,128)S(1)}, f32[6,2304]{1,0:T(8,128)S(1)}, u32[]{:S(2)}, u32[]{:S(2)}) collective-permute-start(f32[6,2304]{1,0:T(8,128)S(1)} %slice.35), channel_id=1, source_target_pairs={{0,32},{1,33},{2,34},{3,35},{4,36},{5,37},{6,38},{7,39},{8,40},{9,... | collective-permute-start | bytes 165896
  835.7 24.8 %collective-permute-start.10 = (f32[8,2304]{1,0:T(8,128)S(1)}, f32[8,2304]{1,0:T(8,128)S(1)}, u32[]{:S(2)}, u32[]{:S(2)}) collective-permute-start(f32[8,2304]{1,0:T(8,128)S(1)} %get-tuple-element.39), channel_id=1, source_target_pairs={{0,11},{1,12},{2,13},{3,14},{4,15},{5,16},{6,17},{7,18},{8,19},{9,... | collective-permute-start | bytes 221192
  840.4 22.5 %collective-permute-start.11 = (f32[8,2304]{1,0:T(8,128)S(1)}, f32[8,2304]{1,0:T(8,128)S(1)}, u32[]{:S(2)}, u32[]{:S(2)}) collective-permute-start(f32[8,2304]{1,0:T(8,128)S(1)} %get-tuple-element.39), channel_id=1, source_target_pairs={{0,12},{1,13},{2,14},{3,15},{4,16},{5,17},{6,18},{7,19},{8,20},{9,... | collective-permute-start | bytes 221192
  845.7 20.6 %collective-permute-start.12 = (f32[8,2304]{1,0:T(8,128)S(1)}, f32[8,2304]{1,0:T(8,128)S(1)}, u32[]{:S(2)}, u32[]{:S(2)}) collective-permute-start(f32[8,2304]{1,0:T(8,128)S(1)} %get-tuple-element.39), channel_id=1, source_target_pairs={{0,13},{1,14},{2,15},{3,16},{4,17},{5,18},{6,19},{7,20},{8,21},{9,... | collective-permute-start | bytes 221192
  851.5 16.9 %collective-permute-start.13 = (f32[8,2304]{1,0:T(8,128)S(1)}, f32[8,2304]{1,0:T(8,128)}, u32[]{:S(2)}, u32[]{:S(2)}) collective-permute-start(f32[8,2304]{1,0:T(8,128)S(1)} %get-tuple-element.39), channel_id=1, source_target_pairs={{0,14},{1,15},{2,16},{3,17},{4,18},{5,19},{6,20},{7,21},{8,22},{9,... | collective-permute-start | bytes 221192
  856.1 15.8 %collective-permute-start.14 = (f32[8,2304]{1,0:T(8,128)S(1)}, f32[8,2304]{1,0:T(8,128)}, u32[]{:S(2)}, u32[]{:S(2)}) collective-permute-start(f32[8,2304]{1,0:T(8,128)S(1)} %get-tuple-element.39), channel_id=1, source_target_pairs={{0,15},{1,16},{2,17},{3,18},{4,19},{5,20},{6,21},{7,22},{8,23},{9,... | collective-permute-start | bytes 221192
  860.5 22.1 %collective-permute-start.15 = (f32[8,2304]{1,0:T(8,128)S(1)}, f32[8,2304]{1,0:T(8,128)S(1)}, u32[]{:S(2)}, u32[]{:S(2)}) collective-permute-start(f32[8,2304]{1,0:T(8,128)S(1)} %get-tuple-element.39), channel_id=1, source_target_pairs={{0,16},{1,17},{2,18},{3,19},{4,20},{5,21},{6,22},{7,23},{8,24},{9,... | collective-permute-start | bytes 221192
  862.9 22.7 %collective-permute-start.16 = (f32[8,2304]{1,0:T(8,128)S(1)}, f32[8,2304]{1,0:T(8,128)S(1)}, u32[]{:S(2)}, u32[]{:S(2)}) collective-permute-start(f32[8,2304]{1,0:T(8,128)S(1)} %get-tuple-element.39), channel_id=1, source_target_pairs={{0,17},{1,18},{2,19},{3,20},{4,21},{5,22},{6,23},{7,24},{8,25},{9,... | collective-permute-start | bytes 221192
  866.3 21.6 %collective-permute-start.17 = (f32[8,2304]{1,0:T(8,128)S(1)}, f32[8,2304]{1,0:T(8,128)S(1)}, u32[]{:S(2)}, u32[]{:S(2)}) collective-permute-start(f32[8,2304]{1,0:T(8,128)S(1)} %get-tuple-element.39), channel_id=1, source_target_pairs={{0,18},{1,19},{2,20},{3,21},{4,22},{5,23},{6,24},{7,25},{8,26},{9,... | collective-permute-start | bytes 221192
  868.3 21.3 %collective-permute-start.18 = (f32[8,2304]{1,0:T(8,128)S(1)}, f32[8,2304]{1,0:T(8,128)S(1)}, u32[]{:S(2)}, u32[]{:S(2)}) collective-permute-start(f32[8,2304]{1,0:T(8,128)S(1)} %get-tuple-element.39), channel_id=1, source_target_pairs={{0,19},{1,20},{2,21},{3,22},{4,23},{5,24},{6,25},{7,26},{8,27},{9,... | collective-permute-start | bytes 221192
  871.9 19.0 %collective-permute-start.19 = (f32[8,2304]{1,0:T(8,128)S(1)}, f32[8,2304]{1,0:T(8,128)S(1)}, u32[]{:S(2)}, u32[]{:S(2)}) collective-permute-start(f32[8,2304]{1,0:T(8,128)S(1)} %get-tuple-element.39), channel_id=1, source_target_pairs={{0,20},{1,21},{2,22},{3,23},{4,24},{5,25},{6,26},{7,27},{8,28},{9,... | collective-permute-start | bytes 221192
  909.8 14.3 %collective-permute-start.30 = (f32[8,2304]{1,0:T(8,128)S(1)}, f32[8,2304]{1,0:T(8,128)S(1)}, u32[]{:S(2)}, u32[]{:S(2)}) collective-permute-start(f32[8,2304]{1,0:T(8,128)S(1)} %get-tuple-element.39), channel_id=1, source_target_pairs={{0,31},{1,32},{2,33},{3,34},{4,35},{5,36},{6,37},{7,38},{8,39},{9,... | collective-permute-start | bytes 221192
  911.1 17.5 %collective-permute-start.4 = (f32[8,2304]{1,0:T(8,128)S(1)}, f32[8,2304]{1,0:T(8,128)S(1)}, u32[]{:S(2)}, u32[]{:S(2)}) collective-permute-start(f32[8,2304]{1,0:T(8,128)S(1)} %get-tuple-element.39), channel_id=1, source_target_pairs={{0,5},{1,6},{2,7},{3,8},{4,9},{5,10},{6,11},{7,12},{8,13},{9,14},{... | collective-permute-start | bytes 221192
  914.8 15.7 %collective-permute-start.5 = (f32[8,2304]{1,0:T(8,128)S(1)}, f32[8,2304]{1,0:T(8,128)S(1)}, u32[]{:S(2)}, u32[]{:S(2)}) collective-permute-start(f32[8,2304]{1,0:T(8,128)S(1)} %get-tuple-element.39), channel_id=1, source_target_pairs={{0,6},{1,7},{2,8},{3,9},{4,10},{5,11},{6,12},{7,13},{8,14},{9,15},... | collective-permute-start | bytes 221192
  917.7 32.3 %collective-permute-start.64 = (f32[8,3072]{1,0:T(8,128)S(1)}, f32[8,3072]{1,0:T(8,128)S(1)}, u32[]{:S(2)}, u32[]{:S(2)}) collective-permute-start(f32[8,3072]{1,0:T(8,128)S(1)} %get-tuple-element.41), channel_id=1, source_target_pairs={{0,1},{1,2},{2,3},{3,4},{4,5},{5,6},{6,7},{7,8},{8,9},{9,10},{10,1... | collective-permute-start | bytes 294920
  920.9 15.7 %collective-permute-start.6 = (f32[8,2304]{1,0:T(8,128)S(1)}, f32[8,2304]{1,0:T(8,128)S(1)}, u32[]{:S(2)}, u32[]{:S(2)}) collective-permute-start(f32[8,2304]{1,0:T(8,128)S(1)} %get-tuple-element.39), channel_id=1, source_target_pairs={{0,7},{1,8},{2,9},{3,10},{4,11},{5,12},{6,13},{7,14},{8,15},{9,16}... | collective-permute-start | bytes 221192
  930.5 15.4 %collective-permute-start.9 = (f32[8,2304]{1,0:T(8,128)S(1)}, f32[8,2304]{1,0:T(8,128)S(1)}, u32[]{:S(2)}, u32[]{:S(2)}) collective-permute-start(f32[8,2304]{1,0:T(8,128)S(1)} %get-tuple-element.39), channel_id=1, source_target_pairs={{0,10},{1,11},{2,12},{3,13},{4,14},{5,15},{6,16},{7,17},{8,18},{9,... | collective-permute-start | bytes 221192
  936.6 15.4 %collective-permute-start.65 = (f32[8,3072]{1,0:T(8,128)S(1)}, f32[8,3072]{1,0:T(8,128)S(1)}, u32[]{:S(2)}, u32[]{:S(2)}) collective-permute-start(f32[8,3072]{1,0:T(8,128)S(1)} %get-tuple-element.41), channel_id=1, source_target_pairs={{0,2},{1,3},{2,4},{3,5},{4,6},{5,7},{6,8},{7,9},{8,10},{9,11},{10,... | collective-permute-start | bytes 294920
  937.9 17.6 %collective-permute-start.66 = (f32[8,3072]{1,0:T(8,128)S(1)}, f32[8,3072]{1,0:T(8,128)S(1)}, u32[]{:S(2)}, u32[]{:S(2)}) collective-permute-start(f32[8,3072]{1,0:T(8,128)S(1)} %get-tuple-element.41), channel_id=1, source_target_pairs={{0,3},{1,4},{2,5},{3,6},{4,7},{5,8},{6,9},{7,10},{8,11},{9,12},{10... | collective-permute-start | bytes 294920
  942.3 14.5 %collective-permute-start.67 = (f32[8,3072]{1,0:T(8,128)S(1)}, f32[8,3072]{1,0:T(8,128)S(1)}, u32[]{:S(2)}, u32[]{:S(2)}) collective-permute-start(f32[8,3072]{1,0:T(8,128)S(1)} %get-tuple-element.41), channel_id=1, source_target_pairs={{0,4},{1,5},{2,6},{3,7},{4,8},{5,9},{6,10},{7,11},{8,12},{9,13},{1... | collective-permute-start | bytes 294920
  975.2 117.3 %collective-permute-start.80 = (f32[8,3072]{1,0:T(8,128)S(1)}, f32[8,3072]{1,0:T(8,128)S(1)}, u32[]{:S(2)}, u32[]{:S(2)}) collective-permute-start(f32[8,3072]{1,0:T(8,128)S(1)} %get-tuple-element.41), channel_id=1, source_target_pairs={{0,17},{1,18},{2,19},{3,20},{4,21},{5,22},{6,23},{7,24},{8,25},{9,... | collective-permute-start | bytes 294920
  978.5 119.1 %collective-permute-start.81 = (f32[8,3072]{1,0:T(8,128)S(1)}, f32[8,3072]{1,0:T(8,128)}, u32[]{:S(2)}, u32[]{:S(2)}) collective-permute-start(f32[8,3072]{1,0:T(8,128)S(1)} %get-tuple-element.41), channel_id=1, source_target_pairs={{0,18},{1,19},{2,20},{3,21},{4,22},{5,23},{6,24},{7,25},{8,26},{9,... | collective-permute-start | bytes 294920
  980.7 121.0 %collective-permute-start.82 = (f32[8,3072]{1,0:T(8,128)S(1)}, f32[8,3072]{1,0:T(8,128)}, u32[]{:S(2)}, u32[]{:S(2)}) collective-permute-start(f32[8,3072]{1,0:T(8,128)S(1)} %get-tuple-element.41), channel_id=1, source_target_pairs={{0,19},{1,20},{2,21},{3,22},{4,23},{5,24},{6,25},{7,26},{8,27},{9,... | collective-permute-start | bytes 294920
  983.5 120.6 %collective-permute-start.83 = (f32[8,3072]{1,0:T(8,128)S(1)}, f32[8,3072]{1,0:T(8,128)}, u32[]{:S(2)}, u32[]{:S(2)}) collective-permute-start(f32[8,3072]{1,0:T(8,128)S(1)} %get-tuple-element.41), channel_id=1, source_target_pairs={{0,20},{1,21},{2,22},{3,23},{4,24},{5,25},{6,26},{7,27},{8,28},{9,... | collective-permute-start | bytes 294920
  985.4 121.3 %collective-permute-start.84 = (f32[8,3072]{1,0:T(8,128)S(1)}, f32[8,3072]{1,0:T(8,128)}, u32[]{:S(2)}, u32[]{:S(2)}) collective-permute-start(f32[8,3072]{1,0:T(8,128)S(1)} %get-tuple-element.41), channel_id=1, source_target_pairs={{0,21},{1,22},{2,23},{3,24},{4,25},{5,26},{6,27},{7,28},{8,29},{9,... | collective-permute-start | bytes 294920
  1092.6 51.9 %collective-permute-start.85 = (f32[8,3072]{1,0:T(8,128)S(1)}, f32[8,3072]{1,0:T(8,128)S(1)}, u32[]{:S(2)}, u32[]{:S(2)}) collective-permute-start(f32[8,3072]{1,0:T(8,128)S(1)} %get-tuple-element.41), channel_id=1, source_target_pairs={{0,22},{1,23},{2,24},{3,25},{4,26},{5,27},{6,28},{7,29},{8,30},{9,... | collective-permute-start | bytes 294920
  1097.5 49.6 %collective-permute-start.86 = (f32[8,3072]{1,0:T(8,128)S(1)}, f32[8,3072]{1,0:T(8,128)S(1)}, u32[]{:S(2)}, u32[]{:S(2)}) collective-permute-start(f32[8,3072]{1,0:T(8,128)S(1)} %get-tuple-element.41), channel_id=1, source_target_pairs={{0,23},{1,24},{2,25},{3,26},{4,27},{5,28},{6,29},{7,30},{8,31},{9,... | collective-permute-start | bytes 294920
  1101.7 48.1 %collective-permute-start.87 = (f32[8,3072]{1,0:T(8,128)S(1)}, f32[8,3072]{1,0:T(8,128)S(1)}, u32[]{:S(2)}, u32[]{:S(2)}) collective-permute-start(f32[8,3072]{1,0:T(8,128)S(1)} %get-tuple-element.41), channel_id=1, source_target_pairs={{0,24},{1,25},{2,26},{3,27},{4,28},{5,29},{6,30},{7,31},{8,32},{9,... | collective-permute-start | bytes 294920
  1104.1 47.3 %collective-permute-start.88 = (f32[8,3072]{1,0:T(8,128)S(1)}, f32[8,3072]{1,0:T(8,128)S(1)}, u32[]{:S(2)}, u32[]{:S(2)}) collective-permute-start(f32[8,3072]{1,0:T(8,128)S(1)} %get-tuple-element.41), channel_id=1, source_target_pairs={{0,25},{1,26},{2,27},{3,28},{4,29},{5,30},{6,31},{7,32},{8,33},{9,... | collective-permute-start | bytes 294920
  1106.7 46.4 %collective-permute-start.89 = (f32[8,3072]{1,0:T(8,128)S(1)}, f32[8,3072]{1,0:T(8,128)S(1)}, u32[]{:S(2)}, u32[]{:S(2)}) collective-permute-start(f32[8,3072]{1,0:T(8,128)S(1)} %get-tuple-element.41), channel_id=1, source_target_pairs={{0,26},{1,27},{2,28},{3,29},{4,30},{5,31},{6,32},{7,33},{8,34},{9,... | collective-permute-start | bytes 294920
  (198 other events, 6854.6 us)
Sparse Core Ops, SparseCore 0:
  10.9 67.8 all-gather.11
  81.8 64.4 all-gather.9
  149.4 65.6 all-gather.13
  218.0 64.7 all-gather.7
  308.5 218.3 reduce-scatter.7
where the time goes:
time: 1210 us; the launch traced here: 1200 us
  blocking collectives  498 us (41%)
  starting transfers between devices  267 us (22%)
  local copies, waits for them, and re-layouts  179 us (15%)
  waiting for transfers between devices  125 us (10%)
  matrix products  97.8 us (8%)
  between operations  18.1 us (1%)
  other arithmetic  13.6 us (1%)
    unnamed x3, blocking collectives  498 us
    unnamed x96, starting transfers between devices  267 us
    unnamed x328, local copies, waits for them, and re-layouts  131 us
    all_gather x1, waiting for transfers between devices, local(): lax.all_gather(attn_local[2], 'fsdp', axis=0, tiled=True)  52.9 us
    dot_general x4, matrix products, mat_product(): return jnp.dot(left, right, preferred_element_type=jnp.float32)  37.8 us
    all_gather x1, waiting for transfers between devices, local(): lax.all_gather(mlp_local[4], 'fsdp', axis=0, tiled=True)  37.7 us
    all_gather x1, waiting for transfers between devices, local(): lax.all_gather(mlp_local[2], 'fsdp', axis=0, tiled=True)  27.3 us
  transfers between devices with their start and end apart: 101, of which 7 were waited for; matrix products, arithmetic and copies ran while one was open for 52% of the time, Pallas kernels for 0%

commit v1 on v0

--- a/solution.py
+++ b/solution.py
@@ -2,6 +2,7 @@
 
 import jax
 import jax.numpy as jnp
+import numpy as np
 from jax import lax
 from jax.sharding import PartitionSpec as P
 
@@ -37,6 +38,176 @@
 
 def column_sums(grad_low):
     return jnp.sum(grad_low, axis=0, dtype=jnp.float32)
+
+
+def torus_perm(axis, offset):
+    grid = np.arange(128).reshape(4, 4, 4, 2)
+    dim = {"z": 0, "y": 1, "x": 2, "core": 3}[axis]
+    return list(zip(grid.reshape(-1).tolist(), np.roll(grid, -offset, dim).reshape(-1).tolist()))
+
+
+def coord(axis):
+    stride, size = {"z": (32, 4), "y": (8, 4), "x": (2, 4), "core": (1, 2)}[axis]
+    return lax.rem(lax.div(lax.axis_index("fsdp"), jnp.int32(stride)), jnp.int32(size))
+
+
+PLANE_GROUPS = np.arange(128).reshape(16, 8).T.tolist()
+
+
+def send(values, axis, offset):
+    return lax.ppermute(values, "fsdp", torus_perm(axis, offset))
+
+
+def up(values):
+    return values.astype(jnp.float32)
+
+
+def down(values):
+    return values.astype(jnp.bfloat16)
+
+
+def block(values, index, dim):
+    return lax.dynamic_index_in_dim(values, index, dim, keepdims=False)
+
+
+def chunks(values, axis, dim):
+    own = coord(axis)
+    return [block(values, lax.rem(own + k, jnp.int32(4)), dim) for k in range(4)]
+
+
+def sum_ring(values, axis, dim):
+    own, one, two, three = chunks(values, axis, dim)
+    half = own.shape[-2] // 16 * 8
+    lo = lambda v: v[..., :half, :]
+    hi = lambda v: v[..., half:, :]
+    fore = send(jnp.concatenate([lo(two), hi(one)], -2), axis, 1)
+    back = send(jnp.concatenate([hi(two), lo(three)], -2), axis, -1)
+    rest = own.shape[-2] - half
+    fore_end = send(down(up(lo(one)) + up(lo(fore))), axis, 1)
+    back_end = send(down(up(hi(three)) + up(back[..., :rest, :])), axis, -1)
+    low = up(lo(own)) + up(back[..., rest:, :]) + up(fore_end)
+    high = up(hi(own)) + up(hi(fore)) + up(back_end)
+    return down(jnp.concatenate([low, high], -2))
+
+
+def sum_direct(values, axis, dim):
+    own, one, two, three = chunks(values, axis, dim)
+    return up(own) + up(send(one, axis, 1)) + up(send(two, axis, 2)) + up(send(three, axis, -1))
+
+
+def pair_grad(left, right):
+    core = coord("core")
+    width = right.shape[1] // 2
+    other = lax.dynamic_slice_in_dim(right, (1 - core) * width, width, 1)
+    mine = lax.dynamic_slice_in_dim(right, core * width, width, 1)
+    arrived = send(down(grad_weight(left, other)), "core", 1)
+    return down(grad_weight(left, mine) + up(arrived))
+
+
+def pair_join(mine, theirs, axis):
+    first = coord("core") == 0
+    return jnp.concatenate([jnp.where(first, mine, theirs), jnp.where(first, theirs, mine)], axis)
+
+
+def early_sums(fc2, fc1, out, small):
+    packed = jnp.concatenate(
+        [
+            fc2.reshape(16, 192, 384),
+            fc1.reshape(16, 48, 4, 384).transpose(0, 2, 1, 3).reshape(16, 192, 384),
+            out.reshape(16, 48, 384),
+            jnp.pad(down(small).reshape(16, 1, 384), ((0, 0), (0, 15), (0, 0))),
+        ],
+        axis=1,
+    ).reshape(16 * 448, 384)
+    part = lax.psum_scatter(
+        packed, "fsdp", scatter_dimension=0, axis_index_groups=PLANE_GROUPS, tiled=True
+    )
+    rows = jnp.concatenate(
+        [
+            part[:192].reshape(4, 48, 384),
+            part[192:384].reshape(4, 4, 12, 384).transpose(1, 0, 2, 3).reshape(4, 48, 384),
+            part[384:432].reshape(4, 12, 384),
+            jnp.pad(part[432].reshape(4, 1, 96), ((0, 0), (0, 3), (0, 288))),
+        ],
+        axis=1,
+    )
+    rows = sum_direct(rows, "x", 0)
+    packed = jnp.concatenate(
+        [
+            rows[:48].reshape(2, 24, 384),
+            rows[48:96].reshape(4, 2, 6, 384).transpose(1, 0, 2, 3).reshape(2, 24, 384),
+            rows[96:108].reshape(2, 6, 384),
+            jnp.pad(rows[108, :96].reshape(2, 1, 48), ((0, 0), (0, 1), (0, 336))),
+        ],
+        axis=1,
+    )
+    core = coord("core")
+    mine = block(packed, core, 0)
+    theirs = send(block(packed, 1 - core, 0), "core", 1)
+    fc2_own = pair_join(mine[:24], theirs[:24], 1)
+    fc1_rows = lambda v: v[24:48].reshape(4, 6, 384).transpose(1, 0, 2).reshape(6, 1536)
+    fc1_own = pair_join(fc1_rows(mine), fc1_rows(theirs), 1)
+    out_own = pair_join(mine[48:54], theirs[48:54], 1)
+    small_own = mine[54, :48] + theirs[54, :48]
+    return fc2_own, fc1_own, out_own, small_own
+
+
+def late_sums(qkv, small):
+    packed = jnp.concatenate(
+        [
+            qkv.reshape(16, 48, 3, 384).transpose(0, 2, 1, 3).reshape(16, 144, 384),
+            jnp.pad(down(small).reshape(16, 1, 192), ((0, 0), (0, 7), (0, 192))),
+        ],
+        axis=1,
+    ).reshape(4, 4, 152, 384)
+    first = down(sum_direct(sum_ring(packed[:, :, :80], "z", 0), "y", 0))
+    second = down(sum_direct(sum_ring(packed[:, :, 80:], "y", 1), "z", 0))
+    part = jnp.concatenate([first, second], 0)
+    rows = jnp.concatenate(
+        [
+            part[:144].reshape(3, 4, 12, 384).transpose(1, 0, 2, 3).reshape(4, 36, 384),
+            jnp.pad(part[144, :192].reshape(4, 1, 48), ((0, 0), (0, 3), (0, 336))),
+        ],
+        axis=1,
+    )
+    rows = sum_direct(rows, "x", 0)
+    packed = jnp.concatenate(
+        [
+            rows[:36].reshape(3, 2, 6, 384).transpose(1, 0, 2, 3).reshape(2, 18, 384),
+            jnp.pad(rows[36, :48].reshape(2, 1, 24), ((0, 0), (0, 5), (0, 360))),
+        ],
+        axis=1,
+    )
+    core = coord("core")
+    mine = block(packed, core, 0)
+    theirs = send(block(packed, 1 - core, 0), "core", 1)
+    qkv_rows = lambda v: v[:18].reshape(3, 6, 384).transpose(1, 0, 2).reshape(6, 1152)
+    return pair_join(qkv_rows(mine), qkv_rows(theirs), 1), mine[18, :24] + theirs[18, :24]
+
+
+def gather_params(ln1_gain, ln1_bias, qkv, qkv_bias, out, out_bias, ln2_gain, ln2_bias, fc1, fc1_bias, fc2, fc2_bias):
+    small = jnp.concatenate(
+        [ln1_gain, ln1_bias, qkv_bias, out_bias, ln2_gain, ln2_bias, fc1_bias, fc2_bias]
+    )
+    packed = jnp.concatenate(
+        [
+            qkv.reshape(6, 3, 768).transpose(1, 0, 2).reshape(18, 768),
+            out,
+            fc1.reshape(6, 4, 768).transpose(1, 0, 2).reshape(24, 768),
+            fc2,
+            jnp.pad(small.reshape(1, 72), ((0, 7), (0, 696))),
+        ],
+        axis=0,
+    )
+    full = lax.all_gather(packed, "fsdp", axis=0, tiled=True).reshape(128, 80, 768)
+    wide = lambda at, n: jnp.concatenate(
+        [full[:, at + 6 * j : at + 6 * j + 6].reshape(768, 768) for j in range(n)], axis=1
+    )
+    vec = lambda at, n: full[:, 72, at : at + n].reshape(128 * n)
+    return (
+        vec(0, 6), vec(6, 6), wide(0, 3), vec(12, 12), wide(18, 1), vec(24, 6),
+        vec(30, 6), vec(36, 6), wide(24, 4), vec(42, 24), full[:, 48:72].reshape(3072, 768), vec(66, 6),
+    )
 
 
 def local(
@@ -59,16 +230,11 @@
     slot_count, seq_len, feature_width = images.shape
     row_count = slot_count * seq_len
     score_scale = 1.0 / math.sqrt(HD)
-    attn_local = (ln1_gain, ln1_bias, qkv_weight, qkv_bias, out_weight, out_bias)
-    mlp_local = (ln2_gain, ln2_bias, fc1_weight, fc1_bias, fc2_weight, fc2_bias)
-    attn_full = (
-        lax.all_gather(attn_local[0], "fsdp", axis=0, tiled=True),
-        lax.all_gather(attn_local[1], "fsdp", axis=0, tiled=True),
-        lax.all_gather(attn_local[2], "fsdp", axis=0, tiled=True),
-        lax.all_gather(attn_local[3], "fsdp", axis=0, tiled=True),
-        lax.all_gather(attn_local[4], "fsdp", axis=0, tiled=True),
-        lax.all_gather(attn_local[5], "fsdp", axis=0, tiled=True),
-    )
+    full = gather_params(
+        ln1_gain, ln1_bias, qkv_weight, qkv_bias, out_weight, out_bias,
+        ln2_gain, ln2_bias, fc1_weight, fc1_bias, fc2_weight, fc2_bias,
+    )
+    attn_full, mlp_full = full[:6], full[6:]
     gain_one, offset_one, qkv_matrix, qkv_offset, out_matrix, out_offset = attn_full
     gain_one = gain_one.astype(jnp.float32)
     offset_one = offset_one.astype(jnp.float32)
@@ -98,14 +264,6 @@
     )
     mixed_low = mixed_heads.reshape(row_count, feature_width).astype(jnp.bfloat16)
     after_attn = inputs + mat_product(mixed_low, out_matrix) + out_offset.astype(jnp.float32)
-    mlp_full = (
-        lax.all_gather(mlp_local[0], "fsdp", axis=0, tiled=True),
-        lax.all_gather(mlp_local[1], "fsdp", axis=0, tiled=True),
-        lax.all_gather(mlp_local[2], "fsdp", axis=0, tiled=True),
-        lax.all_gather(mlp_local[3], "fsdp", axis=0, tiled=True),
-        lax.all_gather(mlp_local[4], "fsdp", axis=0, tiled=True),
-        lax.all_gather(mlp_local[5], "fsdp", axis=0, tiled=True),
-    )
     gain_two = mlp_full[0].astype(jnp.float32)
     offset_two = mlp_full[1].astype(jnp.float32)
     normed_two = normalize(after_attn, gain_two, offset_two).astype(jnp.bfloat16)
@@ -118,46 +276,23 @@
         .reshape(slot_count, seq_len, feature_width)
         .astype(jnp.bfloat16)
     )
-    mlp_back = (
-        lax.all_gather(mlp_local[0], "fsdp", axis=0, tiled=True),
-        lax.all_gather(mlp_local[1], "fsdp", axis=0, tiled=True),
-        lax.all_gather(mlp_local[2], "fsdp", axis=0, tiled=True),
-        lax.all_gather(mlp_local[3], "fsdp", axis=0, tiled=True),
-        lax.all_gather(mlp_local[4], "fsdp", axis=0, tiled=True),
-        lax.all_gather(mlp_local[5], "fsdp", axis=0, tiled=True),
-    )
+    mlp_back = mlp_full
     g_branch_f = d_out.reshape(row_count, feature_width).astype(jnp.float32) * row_live
     g_branch = g_branch_f.astype(jnp.bfloat16)
     d_fc2_bias = column_sums(g_branch)
-    d_fc2_weight = grad_weight(hidden_low, g_branch)
+    fc2_half = pair_grad(hidden_low, g_branch)
     g_hidden = grad_input(g_branch, mlp_back[4])
     g_pre = gelu_back(g_hidden)[0].astype(jnp.bfloat16)
     d_fc1_bias = column_sums(g_pre)
-    d_fc1_weight = grad_weight(normed_two, g_pre)
+    fc1_half = pair_grad(normed_two, g_pre)
     g_normed_two = grad_input(g_pre, mlp_back[2])
     norm_two_back = jax.vjp(normalize, after_attn, gain_two, offset_two)[1]
     g_after_part, d_ln2_gain, d_ln2_bias = norm_two_back(g_normed_two)
     g_after = g_branch_f + g_after_part
-    mlp_grads = (d_ln2_gain, d_ln2_bias, d_fc1_weight, d_fc1_bias, d_fc2_weight, d_fc2_bias)
-    mlp_owned = (
-        lax.psum_scatter(mlp_grads[0], "fsdp", scatter_dimension=0, tiled=True),
-        lax.psum_scatter(mlp_grads[1], "fsdp", scatter_dimension=0, tiled=True),
-        lax.psum_scatter(mlp_grads[2], "fsdp", scatter_dimension=0, tiled=True),
-        lax.psum_scatter(mlp_grads[3], "fsdp", scatter_dimension=0, tiled=True),
-        lax.psum_scatter(mlp_grads[4], "fsdp", scatter_dimension=0, tiled=True),
-        lax.psum_scatter(mlp_grads[5], "fsdp", scatter_dimension=0, tiled=True),
-    )
-    attn_back = (
-        lax.all_gather(attn_local[0], "fsdp", axis=0, tiled=True),
-        lax.all_gather(attn_local[1], "fsdp", axis=0, tiled=True),
-        lax.all_gather(attn_local[2], "fsdp", axis=0, tiled=True),
-        lax.all_gather(attn_local[3], "fsdp", axis=0, tiled=True),
-        lax.all_gather(attn_local[4], "fsdp", axis=0, tiled=True),
-        lax.all_gather(attn_local[5], "fsdp", axis=0, tiled=True),
-    )
+    attn_back = attn_full
     g_attn = g_after.astype(jnp.bfloat16)
     d_out_bias = column_sums(g_attn)
-    d_out_weight = grad_weight(mixed_low, g_attn)
+    out_half = pair_grad(mixed_low, g_attn)
     g_mixed = (
         grad_input(g_attn, attn_back[4]).astype(jnp.bfloat16).reshape(slot_count, seq_len, H, HD)
     )
@@ -195,37 +330,23 @@
     ).astype(jnp.bfloat16)
     qkv_sums = column_sums(g_qkv)
     d_qkv_bias = jnp.concatenate([qkv_sums[:feature_width], qkv_sums[2 * feature_width :]])
-    d_qkv_weight = grad_weight(normed_one, g_qkv)
+    qkv_half = pair_grad(normed_one, g_qkv)
     g_normed_one = grad_input(g_qkv, attn_back[2])
     norm_one_back = jax.vjp(normalize, inputs, gain_one, offset_one)[1]
     g_input_part, d_ln1_gain, d_ln1_bias = norm_one_back(g_normed_one)
     d_images = (
         (g_after + g_input_part).reshape(slot_count, seq_len, feature_width).astype(jnp.bfloat16)
     )
-    attn_grads = (d_ln1_gain, d_ln1_bias, d_qkv_weight, d_qkv_bias, d_out_weight, d_out_bias)
-    attn_owned = (
-        lax.psum_scatter(attn_grads[0], "fsdp", scatter_dimension=0, tiled=True),
-        lax.psum_scatter(attn_grads[1], "fsdp", scatter_dimension=0, tiled=True),
-        lax.psum_scatter(attn_grads[2], "fsdp", scatter_dimension=0, tiled=True),
-        lax.psum_scatter(attn_grads[3], "fsdp", scatter_dimension=0, tiled=True),
-        lax.psum_scatter(attn_grads[4], "fsdp", scatter_dimension=0, tiled=True),
-        lax.psum_scatter(attn_grads[5], "fsdp", scatter_dimension=0, tiled=True),
-    )
+    per = lambda v: v.reshape(128, -1)
+    small_early = jnp.concatenate(
+        [per(d_out_bias), per(d_ln2_gain), per(d_ln2_bias), per(d_fc1_bias), per(d_fc2_bias)], 1
+    )
+    small_late = jnp.concatenate([per(d_ln1_gain), per(d_ln1_bias), per(d_qkv_bias)], 1)
+    d_fc2, d_fc1, d_out_w, early = early_sums(fc2_half, fc1_half, out_half, small_early)
+    d_qkv, late = late_sums(qkv_half, small_late)
     return (
-        out_images,
-        d_images,
-        attn_owned[0],
-        attn_owned[1],
-        attn_owned[2],
-        attn_owned[3],
-        attn_owned[4],
-        attn_owned[5],
-        mlp_owned[0],
-        mlp_owned[1],
-        mlp_owned[2],
-        mlp_owned[3],
-        mlp_owned[4],
-        mlp_owned[5],
+        out_images, d_images, late[:6], late[6:12], d_qkv, late[12:24], d_out_w, early[:6],
+        early[6:12], early[12:18], d_fc1, early[18:42], d_fc2, early[42:48],
     )
 
 

time: 1210 us -> 440 us (0.36)
  blocking collectives: 498 us -> 0 us
  starting transfers between devices: 267 us -> 39.3 us
  waiting for transfers between devices: 125 us -> 96.8 us
  local copies, waits for them, and re-layouts: 179 us -> 154 us
  other arithmetic: 13.6 us -> 34.1 us
    unnamed x3 -> x0, blocking collectives: 498 us -> none
    unnamed x96 -> x0, starting transfers between devices: 267 us -> none
    unnamed x328 -> x136, local copies, waits for them, and re-layouts: 131 us -> 20.6 us
    all_gather x4 -> x1, waiting for transfers between devices: 118 us -> 71.1 us  [gather_params(): lax.all_gather(packed, 'fsdp', axis=0, tiled=True).reshape(128, 80, 768)]
    ppermute x0 -> x26, starting transfers between devices: none -> 39.2 us  [send(): return lax.ppermute(values, 'fsdp', torus_perm(axis, offset))]
    reshape x0 -> x34, local copies, waits for them, and re-layouts: none -> 34.6 us  [the longest x8 23.7 us: gather_params(): full[:, at + 6 * j:at + 6 * j + 6].reshape(768, 768)]
    slice x0 -> x28, local copies, waits for them, and re-layouts: none -> 23.8 us  [the longest x1 11.4 us: gather_params(): full[:, at + 6 * j:at + 6 * j + 6].reshape(768, 768)]
    ppermute x0 -> x26, waiting for transfers between devices: none -> 21.4 us  [send(): return lax.ppermute(values, 'fsdp', torus_perm(axis, offset))]
  transfers between devices with their start and end apart: 101 -> 28, of which waited for: 7 -> 15; matrix products, arithmetic and copies ran while one was open for 52% -> 16% of each run, Pallas kernels for 0% -> 0%
where the time goes in v1:
time: 440 us; the launch traced here: 434 us
  local copies, waits for them, and re-layouts  154 us (35%)
  waiting for transfers between devices  96.8 us (22%)
  matrix products  93.3 us (21%)
  starting transfers between devices  39.3 us (9%)
  other arithmetic  34.1 us (8%)
  between operations  16.4 us (4%)
    all_gather x1, waiting for transfers between devices, gather_params(): lax.all_gather(packed, 'fsdp', axis=0, tiled=True).reshape(128, 80, 768)  71.1 us
    ppermute x26, starting transfers between devices, send(): return lax.ppermute(values, 'fsdp', torus_perm(axis, offset))  39.2 us
    dot_general x8, matrix products, grad_weight(): jnp.einsum('ra,rb->ab', left, right, preferred_element_type=jnp.float32)  30.8 us
    dot_general x4, matrix products, grad_input(): jnp.einsum('rb,ab->ra', grad_low, matrix, preferred_element_type=jnp.floa...  29.9 us
    reshape x8, local copies, waits for them, and re-layouts, gather_params(): full[:, at + 6 * j:at + 6 * j + 6].reshape(768, 768)  23.7 us
    ppermute x26, waiting for transfers between devices, send(): return lax.ppermute(values, 'fsdp', torus_perm(axis, offset))  21.4 us
    unnamed x136, local copies, waits for them, and re-layouts  20.6 us
    dot_general x4, matrix products, mat_product(): return jnp.dot(left, right, preferred_element_type=jnp.float32)  17.8 us
  transfers between devices with their start and end apart: 28, of which 15 were waited for; matrix products, arithmetic and copies ran while one was open for 16% of the time, Pallas kernels for 0%

profile of v1, /device:TPU:1, one launch (start us, length us, event | category | flops | bytes accessed | tf_op | source)
XLA Modules:
  0.0 433.7 jit_solution(2070210134192620764)
XLA Ops:
  8.9 5.4 %concatenate.94 = bf16[72]{0:T(256)(128)(2,1)S(1)} concatenate(bf16[6]{0:T(256)(128)(2,1)} %param.17, bf16[6]{0:T(256)(128)(2,1)} %param.18, bf16[12]{0:T(256)(128)(2,1)} %param.20, bf16[6]{0:T(256)(128)(2,1)} %param.22, bf16[6]{0:T(256)(128)(2,1)} %param.23, bf16[6]{0:T(256)(128)(2,1)} %param.24, bf16[24]{0:T(256)(128)(2,1)} %param.26, bf16[6]{0:T(256)(128)(2,1)} %param.28), dimensions={0} | concatenate | bytes 288 | tf_op jit(solution)/shard_map/concatenate | solution.py:189
  14.4 4.6 %concatenate.95 = bf16[80,768]{1,0:T(8,128)(2,1)} concatenate(bf16[18,768]{1,0:T(8,128)(2,1)S(1)} %reshape.457, bf16[6,768]{1,0:T(8,128)(2,1)} %param.21, bf16[24,768]{1,0:T(8,128)(2,1)S(1)} %reshape.459, bf16[24,768]{1,0:T(8,128)(2,1)} %param.27, bf16[8,768]{1,0:T(8,128)(2,1)S(1)} %pad.28), dimensions={0} | concatenate | bytes 245760 | tf_op jit(solution)/shard_map/concatenate | solution.py:192
  30.0 71.1 %all-gather.2.cloned.1.call-done = bf16[10240,768]{1,0:T(8,128)(2,1)} async-done(((bf16[80,768]{1,0:T(8,128)(2,1)}), bf16[10240,768]{1,0:T(8,128)(2,1)}) %all-gather.2.cloned.1.call-update) | async-done | bytes 15728656 | tf_op jit(solution)/shard_map/all_gather | solution.py:202
  104.0 3.6 fusion.58
  107.6 4.8 %slice.407 = bf16[128,24,768]{2,1,0:T(8,128)(2,1)} slice(bf16[128,80,768]{2,1,0:T(8,128)(2,1)} %bitcast.202), slice={[0:128], [48:72], [0:768]} | slice | bytes 9437184 | tf_op jit(solution)/shard_map/slice | solution.py:209
  112.4 11.4 %fusion.103 = (bf16[128,6,768]{2,1,0:T(8,128)(2,1)}, bf16[128,6,768]{2,1,0:T(8,128)(2,1)}, bf16[128,6,768]{2,1,0:T(8,128)(2,1)}, bf16[128,6,768]{2,1,0:T(8,128)(...) fusion(bf16[128,80,768]{2,1,0:T(8,128)(2,1)} %bitcast.203), kind=kLoop, calls=%fused_computation.263 | loop fusion | bytes 18874368 | tf_op jit(solution)/shard_map/slice | solution.py:204
  131.3 3.2 reshape.472
  134.5 3.2 reshape.468
  137.7 3.2 reshape.470
  140.9 3.2 reshape.469
  144.1 3.2 reshape.471
  147.3 3.2 reshape.464
  150.5 3.2 reshape.463
  162.1 4.0 reshape.524
  166.1 4.2 copy.178
  170.3 4.0 reshape.523
  174.3 4.2 copy.177
  178.5 2.9 reshape.522
  181.4 3.5 copy.179
  185.0 2.8 constant_dynamic-update-slice_fusion.6
  187.8 2.8 multiply_reduce_fusion.1
  198.3 2.7 fusion.109
  205.9 5.4 %fusion.110 = f32[591,3072]{1,0:T(8,128)S(1)} fusion(bf16[591,768]{1,0:T(8,128)(2,1)S(1)} %add_convert_fusion.6, bf16[768,3072]{1,0:T(8,128)(2,1)} %constant_dynamic-update-slice_fusion.3), kind=kOutput, calls=%fused_computation.271 | convolution fusion | flops 2788687872 | bytes 12888576 | tf_op jit(solution)/shard_map/dot_general | solution.py:28
  211.4 22.1 %fusion.97 = (bf16[3072]{0:T(1024)(128)(2,1)}, bf16[591,3072]{1,0:T(8,128)(2,1)S(1)}, f32[591,3072]{1,0:T(8,128)}) fusion(f32[591,3072]{1,0:T(8,128)S(1)} %fusion.110, f32[3072]{0:T(1024)S(1)} %copy-done.39, bf16[591,768]{1,0:T(8,128)(2,1)S(1)} %copy-done.29, bf16[3072,768]{1,0:T(8,128)(2,1)S(1)} %bitcast.213), kind=kOutput, calls=%fused_computation.259 | convolution fusion | flops 2923035648 | bytes 23800320 | tf_op jit(solution)/shard_map/rb,ab->ra/dot_general | solution.py:36
  233.5 3.9 multiply_reduce_fusion.3
  241.2 2.9 reshape.525
  244.1 4.4 %copy.185 = bf16[3,197,12,64]{1,3,2,0:T(8,128)(2,1)} copy(bf16[3,197,12,64]{3,2,1,0:T(8,128)(2,1)} %reshape.525) | data formatting | bytes 1815552 | tf_op jit(solution)/shard_map/reshape | solution.py:297
  248.5 5.0 %fusion.22 = bf16[3,197,12,64]{1,3,2,0:T(8,128)(2,1)S(1)} fusion(bf16[3,197,12,64]{1,3,2,0:T(8,128)(2,1)} %copy.185, f32[3,12,197,197]{2,3,1,0:T(8,128)} %copy-done, f32[3,12,197]{2,1,0:T(8,128)S(1)} %log_add_fusion), kind=kOutput, calls=%fused_computation.67 | convolution fusion | flops 183477136 | bytes 7432416 | tf_op jit(solution)/shard_map/ghqk,gqhd->gkhd/dot_general | solution.py:307
  261.7 8.7 %multiply_convert_fusion.1 = bf16[591,3072]{1,0:T(8,128)(2,1)} fusion(f32[591,3072]{1,0:T(8,128)} %get-tuple-element.31, f32[591,3072]{1,0:T(8,128)} %copy-done.15, f32[3072]{0:T(1024)S(1)} %copy-done.39), kind=kLoop, calls=%fused_computation.9 | loop fusion | flops 7262208 | bytes 18167808 | tf_op jit(solution)/shard_map/convert_element_type | solution.py:272
  273.5 5.3 %convolution_convert_fusion.1 = bf16[768,1536]{1,0:T(8,128)(2,1)} fusion(bf16[591,768]{1,0:T(8,128)(2,1)} %copy-done.31, bf16[591,3072]{1,0:T(8,128)(2,1)} %copy-done.54, s32[]{:T(128)S(6)} %select_n.195), kind=kOutput, calls=%fused_computation.31 | convolution fusion | flops 1395523584 | bytes 5087236 | tf_op jit(solution)/shard_map/ra,rb->ab/dot_general | solution.py:32
  287.7 2.9 multiply_reduce_fusion.4
  295.1 3.8 convolution_convert_fusion
  302.0 2.7 collective-permute-done.21
  306.4 5.6 %add_convert_fusion.2 = bf16[768,1536]{1,0:T(8,128)(2,1)} fusion(bf16[768,1536]{1,0:T(8,128)(2,1)} %collective-permute-done.20, bf16[591,768]{1,0:T(8,128)(2,1)S(1)} %copy-done.32, bf16[591,3072]{1,0:T(8,128)(2,1)} %copy-done.54, s32[]{:T(128)S(6)} %select_n.194), kind=kOutput, calls=%fused_computation.27 | convolution fusion | flops 1397882880 | bytes 7444996 | tf_op jit(solution)/shard_map/ra,rb->ab/dot_general | solution.py:32
  312.1 4.5 %reshape.488 = bf16[16,48,4,384]{3,2,1,0:T(4,128)(2,1)S(1)} reshape(bf16[768,1536]{1,0:T(8,128)(2,1)} %add_convert_fusion.2) | data formatting | bytes 4718592 | tf_op jit(solution)/shard_map/reshape | solution.py:116
  318.9 4.0 add_convert_fusion.3
  322.9 3.3 fusion.7
  328.1 4.1 convolution_convert_fusion.2
  336.2 4.7 %add_convert_fusion.4 = bf16[768,1152]{1,0:T(8,128)(2,1)} fusion(bf16[768,1152]{1,0:T(8,128)(2,1)} %collective-permute-done, bf16[591,768]{1,0:T(8,128)(2,1)} %copy-done.30, bf16[591,2304]{0,1:T(8,128)(2,1)S(1)} %copy-done.17, s32[]{:T(128)S(6)} %select_n.168), kind=kOutput, calls=%fused_computation.30 | convolution fusion | flops 1048412160 | bytes 5921284 | tf_op jit(solution)/shard_map/ra,rb->ab/dot_general | solution.py:32
  340.9 3.3 reshape.478
  350.9 5.3 %collective-permute-done.9 = bf16[4,72,384]{2,1,0:T(8,128)(2,1)S(1)} collective-permute-done((bf16[4,72,384]{2,1,0:T(8,128)(2,1)S(1)}, bf16[4,72,384]{2,1,0:T(8,128)(2,1)S(1)}, u32[]{:S(2)}, u32[]{:S(2)}) %collective-permute-start.9) | collective-permute-done | bytes 221216 | tf_op jit(solution)/shard_map/ppermute | solution.py:58
  370.0 3.7 collective-permute-start.6
  378.2 3.5 collective-permute-start.16
  386.3 5.1 %collective-permute-start.18 = (f32[24,384]{1,0:T(8,128)S(1)}, f32[24,384]{1,0:T(8,128)S(1)}, u32[]{:S(2)}, u32[]{:S(2)}) collective-permute-start(f32[24,384]{1,0:T(8,128)S(1)} %bitcast.239), channel_id=1, source_target_pairs={{0,1},{1,0},{2,3},{3,2},{4,5},{5,4},{6,7},{7,6},{8,9},{9,8},{10,11... | collective-permute-start | bytes 110600 | tf_op jit(solution)/shard_map/ppermute | solution.py:58
  391.4 7.3 %multiply_convert_fusion.5 = bf16[591,768]{1,0:T(8,128)(2,1)} fusion(f32[591,768]{1,0:T(8,128)S(1)} %copy-done.2, bf16[591,3072]{1,0:T(8,128)(2,1)} %multiply_convert_fusion.1, bf16[3072,768]{1,0:T(8,128)(2,1)} %bitcast.210, f32[591]{0:T(1024)S(1)} %copy-done.44, f32[768]{0:T(1024)S(1)} %reshape.516), kind=kOutput, calls=%fused_computation.48 | convolution fusion | flops 2790503424 | bytes 11078460 | tf_op jit(solution)/shard_map/dot_general | solution.py:28
  403.6 4.3 reduce-scatter.2.cloned.1.call-done
  415.6 3.5 collective-permute-done.23
  419.8 2.7 collective-permute-start.25
  (366 shorter events, 130.6 us)
Async XLA Ops:
  7.2 14.6 %copy-start.14 = (bf16[3,197,768]{2,1,0:T(8,128)(2,1)S(1)}, bf16[3,197,768]{2,1,0:T(8,128)(2,1)}, u32[]{:S(2)}) copy-start(bf16[3,197,768]{2,1,0:T(8,128)(2,1)} %param.15) | copy-start | bytes 2723332
  7.2 93.9 %all-gather.2.cloned.1.call-start = ((), (), s32[]{:S(2)}) async-start(), calls=%async_computation.1 | async-start | bytes 15851520 | tf_op jit(solution)/shard_map/all_gather | solution.py:202
  18.9 388.9 %reduce-scatter.2.cloned.1.call-start = ((), (), s32[]{:S(2)}) async-start(), calls=%async_computation.2 | async-start | bytes 5849088 | tf_op jit(solution)/shard_map/reduce_scatter | solution.py:122
  21.8 176.5 %copy-start.3 = (f32[591,768]{1,0:T(8,128)}, f32[591,768]{1,0:T(8,128)S(1)}, u32[]{:S(2)}) copy-start(f32[591,768]{1,0:T(8,128)S(1)} %reshape.507) | copy-start | bytes 5446660
  184.9 7.2 %copy-start.9 = (bf16[3,197,12,64]{1,3,2,0:T(8,128)(2,1)}, bf16[3,197,12,64]{1,3,2,0:T(8,128)(2,1)S(1)}, u32[]{:S(2)}) copy-start(bf16[3,197,12,64]{1,3,2,0:T(8,128)(2,1)S(1)} %copy.179) | copy-start | bytes 2723332
  201.0 36.4 %copy-start.1 = (f32[591,768]{1,0:T(8,128)}, f32[591,768]{1,0:T(8,128)S(1)}, u32[]{:S(2)}) copy-start(f32[591,768]{1,0:T(8,128)S(1)} %get-tuple-element.106) | copy-start | bytes 5446660
  205.5 5.8 %slice-start.2 = ((s8[4718592]{0:T(1024)(128)(4,1)}), s8[4194304]{0:T(1024)(128)(4,1)S(1)}, s32[]{:S(2)}) async-start(s8[4718592]{0:T(1024)(128)(4,1)} %bitcast.211), calls=%async_computation.5 | async-start | bytes 8388608
  205.8 5.5 %slice-start.3 = ((s8[4718592]{0:T(1024)(128)(4,1)}), s8[524288]{0:T(1024)(128)(4,1)S(1)}, s32[]{:S(2)}) async-start(s8[4718592]{0:T(1024)(128)(4,1)} %bitcast.211), calls=%async_computation.6 | async-start | bytes 1048576
  205.8 5.5 %copy-start.29 = (bf16[591,768]{1,0:T(8,128)(2,1)S(1)}, bf16[591,768]{1,0:T(8,128)(2,1)}, u32[]{:S(2)}) copy-start(bf16[591,768]{1,0:T(8,128)(2,1)} %convert_element_type.427) | copy-start | bytes 2723332
  205.9 27.6 %slice-start.4 = ((s8[4718592]{0:T(1024)(128)(4,1)}), s8[524288]{0:T(1024)(128)(4,1)S(1)}, s32[]{:S(2)}) async-start(s8[4718592]{0:T(1024)(128)(4,1)} %bitcast.223), calls=%async_computation.7 | async-start | bytes 1048576
  211.3 22.2 %copy-start.15 = (f32[591,3072]{1,0:T(8,128)}, f32[591,3072]{1,0:T(8,128)S(1)}, u32[]{:S(2)}) copy-start(f32[591,3072]{1,0:T(8,128)S(1)} %fusion.110) | copy-start | bytes 21786628
  211.3 22.1 %slice-start.5 = ((s8[4718592]{0:T(1024)(128)(4,1)}), s8[4194304]{0:T(1024)(128)(4,1)S(1)}, s32[]{:S(2)}) async-start(s8[4718592]{0:T(1024)(128)(4,1)} %bitcast.223), calls=%async_computation.8 | async-start | bytes 8388608
  244.1 9.4 %slice-start = ((s8[7372800]{0:T(1024)(128)(4,1)}), s8[3178496]{0:T(1024)(128)(4,1)S(1)}, s32[]{:S(2)}) async-start(s8[7372800]{0:T(1024)(128)(4,1)} %bitcast.196), calls=%async_computation.3 | async-start | bytes 6356992
  273.5 5.5 %copy-start.22 = (bf16[3,197,12,64]{1,3,2,0:T(8,128)(2,1)S(1)}, bf16[3,197,12,64]{1,3,2,0:T(8,128)(2,1)}, u32[]{:S(2)}) copy-start(bf16[3,197,12,64]{1,3,2,0:T(8,128)(2,1)} %fusion.19) | copy-start | bytes 2723332
  278.8 27.6 %collective-permute-start.20 = (bf16[768,1536]{1,0:T(8,128)(2,1)}, bf16[768,1536]{1,0:T(8,128)(2,1)}, u32[]{:S(2)}, u32[]{:S(2)}) collective-permute-start(bf16[768,1536]{1,0:T(8,128)(2,1)} %convolution_convert_fusion.1), channel_id=1, source_target_pairs={{0,1},{1,0},{2,3},{3,2},{4,5},{5,4},{6,7},{7,6},{8,9},{9,8},{10,11... | collective-permute-start | bytes 7077896 | tf_op jit(solution)/shard_map/ppermute | solution.py:58
  295.1 5.9 %copy-start.49 = (bf16[768]{0:T(1024)(128)(2,1)S(1)}, bf16[768]{0:T(1024)(128)(2,1)}, u32[]{:S(2)}) copy-start(bf16[768]{0:T(1024)(128)(2,1)} %get-tuple-element.27) | copy-start | bytes 4612
  295.1 6.0 %copy-start.51 = (bf16[3072]{0:T(1024)(128)(2,1)S(1)}, bf16[3072]{0:T(1024)(128)(2,1)}, u32[]{:S(2)}) copy-start(bf16[3072]{0:T(1024)(128)(2,1)} %get-tuple-element.29) | copy-start | bytes 18436
  295.1 6.1 %copy-start.53 = (bf16[768]{0:T(1024)(128)(2,1)S(1)}, bf16[768]{0:T(1024)(128)(2,1)}, u32[]{:S(2)}) copy-start(bf16[768]{0:T(1024)(128)(2,1)} %get-tuple-element.21) | copy-start | bytes 4612
  295.1 6.3 %copy-start.52 = (bf16[768]{0:T(1024)(128)(2,1)S(1)}, bf16[768]{0:T(1024)(128)(2,1)}, u32[]{:S(2)}) copy-start(bf16[768]{0:T(1024)(128)(2,1)} %get-tuple-element.25) | copy-start | bytes 4612
  295.1 6.4 %copy-start.50 = (bf16[768]{0:T(1024)(128)(2,1)S(1)}, bf16[768]{0:T(1024)(128)(2,1)}, u32[]{:S(2)}) copy-start(bf16[768]{0:T(1024)(128)(2,1)} %get-tuple-element.32) | copy-start | bytes 4612
  298.9 7.5 %copy-start.32 = (bf16[591,768]{1,0:T(8,128)(2,1)S(1)}, bf16[591,768]{1,0:T(8,128)(2,1)}, u32[]{:S(2)}) copy-start(bf16[591,768]{1,0:T(8,128)(2,1)} %copy-done.31) | copy-start | bytes 2723332
  298.9 18.1 %collective-permute-start.19 = (bf16[3072,384]{1,0:T(8,128)(2,1)}, bf16[3072,384]{1,0:T(8,128)(2,1)}, u32[]{:S(2)}, u32[]{:S(2)}) collective-permute-start(bf16[3072,384]{1,0:T(8,128)(2,1)} %convolution_convert_fusion), channel_id=1, source_target_pairs={{0,1},{1,0},{2,3},{3,2},{4,5},{5,4},{6,7},{7,6},{8,9},{9,8},{10,11... | collective-permute-start | bytes 7077896 | tf_op jit(solution)/shard_map/ppermute | solution.py:58
  300.7 3.9 collective-permute-start.21
  332.2 4.0 collective-permute-start
  345.1 11.0 %collective-permute-start.9 = (bf16[4,72,384]{2,1,0:T(8,128)(2,1)S(1)}, bf16[4,72,384]{2,1,0:T(8,128)(2,1)S(1)}, u32[]{:S(2)}, u32[]{:S(2)}) collective-permute-start(bf16[4,72,384]{2,1,0:T(8,128)(2,1)S(1)} %pad_maximum_fusion.3), channel_id=1, source_target_pairs={{0,8},{1,9},{2,10},{3,11},{4,12},{5,13},{6,14},{7,15},{8,16},{9,17... | collective-permute-start | bytes 663560 | tf_op jit(solution)/shard_map/ppermute | solution.py:58
  346.4 10.6 %collective-permute-start.8 = (bf16[4,72,384]{2,1,0:T(8,128)(2,1)S(1)}, bf16[4,72,384]{2,1,0:T(8,128)(2,1)S(1)}, u32[]{:S(2)}, u32[]{:S(2)}) collective-permute-start(bf16[4,72,384]{2,1,0:T(8,128)(2,1)S(1)} %pad_maximum_fusion.2), channel_id=1, source_target_pairs={{0,24},{1,25},{2,26},{3,27},{4,28},{5,29},{6,30},{7,31},{8,0},{9,1... | collective-permute-start | bytes 663560 | tf_op jit(solution)/shard_map/ppermute | solution.py:58
  348.0 12.3 %collective-permute-start.2 = (bf16[4,80,384]{2,1,0:T(8,128)(2,1)S(1)}, bf16[4,80,384]{2,1,0:T(8,128)(2,1)S(1)}, u32[]{:S(2)}, u32[]{:S(2)}) collective-permute-start(bf16[4,80,384]{2,1,0:T(8,128)(2,1)S(1)} %pad_maximum_fusion.1), channel_id=1, source_target_pairs={{0,32},{1,33},{2,34},{3,35},{4,36},{5,37},{6,38},{7,39},{8,40},{9,... | collective-permute-start | bytes 737288 | tf_op jit(solution)/shard_map/ppermute | solution.py:58
  348.9 12.2 %collective-permute-start.1 = (bf16[4,80,384]{2,1,0:T(8,128)(2,1)S(1)}, bf16[4,80,384]{2,1,0:T(8,128)(2,1)S(1)}, u32[]{:S(2)}, u32[]{:S(2)}) collective-permute-start(bf16[4,80,384]{2,1,0:T(8,128)(2,1)S(1)} %pad_maximum_fusion), channel_id=1, source_target_pairs={{0,96},{1,97},{2,98},{3,99},{4,100},{5,101},{6,102},{7,103},{8,104... | collective-permute-start | bytes 737288 | tf_op jit(solution)/shard_map/ppermute | solution.py:58
  356.2 7.0 %collective-permute-start.10 = (bf16[4,32,384]{2,1,0:T(8,128)(2,1)S(1)}, bf16[4,32,384]{2,1,0:T(8,128)(2,1)S(1)}, u32[]{:S(2)}, u32[]{:S(2)}) collective-permute-start(bf16[4,32,384]{2,1,0:T(8,128)(2,1)S(1)} %add_convert_fusion.16), channel_id=1, source_target_pairs={{0,8},{1,9},{2,10},{3,11},{4,12},{5,13},{6,14},{7,15},{8,16},{9,17... | collective-permute-start | bytes 294920 | tf_op jit(solution)/shard_map/ppermute | solution.py:58
  357.1 34.3 %copy-start.2 = (f32[591,768]{1,0:T(8,128)S(1)}, f32[591,768]{1,0:T(8,128)}, u32[]{:S(2)}) copy-start(f32[591,768]{1,0:T(8,128)} %copy-done.1) | copy-start | bytes 5446660
  357.1 7.1 %collective-permute-start.11 = (bf16[4,40,384]{2,1,0:T(8,128)(2,1)S(1)}, bf16[4,40,384]{2,1,0:T(8,128)(2,1)S(1)}, u32[]{:S(2)}, u32[]{:S(2)}) collective-permute-start(bf16[4,40,384]{2,1,0:T(8,128)(2,1)S(1)} %add_convert_fusion.10), channel_id=1, source_target_pairs={{0,24},{1,25},{2,26},{3,27},{4,28},{5,29},{6,30},{7,31},{8,0},{9,1... | collective-permute-start | bytes 368648 | tf_op jit(solution)/shard_map/ppermute | solution.py:58
  360.3 8.6 %collective-permute-start.3 = (bf16[4,40,384]{2,1,0:T(8,128)(2,1)S(1)}, bf16[4,40,384]{2,1,0:T(8,128)(2,1)S(1)}, u32[]{:S(2)}, u32[]{:S(2)}) collective-permute-start(bf16[4,40,384]{2,1,0:T(8,128)(2,1)S(1)} %add_convert_fusion.14), channel_id=1, source_target_pairs={{0,32},{1,33},{2,34},{3,35},{4,36},{5,37},{6,38},{7,39},{8,40},{9,... | collective-permute-start | bytes 368648 | tf_op jit(solution)/shard_map/ppermute | solution.py:58
  361.2 7.7 %collective-permute-start.4 = (bf16[4,40,384]{2,1,0:T(8,128)(2,1)S(1)}, bf16[4,40,384]{2,1,0:T(8,128)(2,1)S(1)}, u32[]{:S(2)}, u32[]{:S(2)}) collective-permute-start(bf16[4,40,384]{2,1,0:T(8,128)(2,1)S(1)} %add_convert_fusion.12), channel_id=1, source_target_pairs={{0,96},{1,97},{2,98},{3,99},{4,100},{5,101},{6,102},{7,103},{8,104... | collective-permute-start | bytes 368648 | tf_op jit(solution)/shard_map/ppermute | solution.py:58
  364.3 9.4 %collective-permute-start.12 = (bf16[72,384]{1,0:T(8,128)(2,1)S(1)}, bf16[72,384]{1,0:T(8,128)(2,1)S(1)}, u32[]{:S(2)}, u32[]{:S(2)}) collective-permute-start(bf16[72,384]{1,0:T(8,128)(2,1)S(1)} %get-tuple-element.71), channel_id=1, source_target_pairs={{0,32},{1,33},{2,34},{3,35},{4,36},{5,37},{6,38},{7,39},{8,40},{9,... | collective-permute-start | bytes 165896 | tf_op jit(solution)/shard_map/ppermute | solution.py:58
  365.5 8.7 %collective-permute-start.13 = (bf16[72,384]{1,0:T(8,128)(2,1)S(1)}, bf16[72,384]{1,0:T(8,128)(2,1)S(1)}, u32[]{:S(2)}, u32[]{:S(2)}) collective-permute-start(bf16[72,384]{1,0:T(8,128)(2,1)S(1)} %get-tuple-element.72), channel_id=1, source_target_pairs={{0,64},{1,65},{2,66},{3,67},{4,68},{5,69},{6,70},{7,71},{8,72},{9,... | collective-permute-start | bytes 165896 | tf_op jit(solution)/shard_map/ppermute | solution.py:58
  367.6 6.7 %collective-permute-start.14 = (bf16[72,384]{1,0:T(8,128)(2,1)S(1)}, bf16[72,384]{1,0:T(8,128)(2,1)S(1)}, u32[]{:S(2)}, u32[]{:S(2)}) collective-permute-start(bf16[72,384]{1,0:T(8,128)(2,1)S(1)} %get-tuple-element.73), channel_id=1, source_target_pairs={{0,96},{1,97},{2,98},{3,99},{4,100},{5,101},{6,102},{7,103},{8,104... | collective-permute-start | bytes 165896 | tf_op jit(solution)/shard_map/ppermute | solution.py:58
  369.0 6.0 %collective-permute-start.5 = (bf16[80,384]{1,0:T(8,128)(2,1)S(1)}, bf16[80,384]{1,0:T(8,128)(2,1)S(1)}, u32[]{:S(2)}, u32[]{:S(2)}) collective-permute-start(bf16[80,384]{1,0:T(8,128)(2,1)S(1)} %get-tuple-element.64), channel_id=1, source_target_pairs={{0,8},{1,9},{2,10},{3,11},{4,12},{5,13},{6,14},{7,15},{8,16},{9,17... | collective-permute-start | bytes 184328 | tf_op jit(solution)/shard_map/ppermute | solution.py:58
  370.0 7.3 %collective-permute-start.6 = (bf16[80,384]{1,0:T(8,128)(2,1)S(1)}, bf16[80,384]{1,0:T(8,128)(2,1)S(1)}, u32[]{:S(2)}, u32[]{:S(2)}) collective-permute-start(bf16[80,384]{1,0:T(8,128)(2,1)S(1)} %get-tuple-element.65), channel_id=1, source_target_pairs={{0,16},{1,17},{2,18},{3,19},{4,20},{5,21},{6,22},{7,23},{8,24},{9,... | collective-permute-start | bytes 184328 | tf_op jit(solution)/shard_map/ppermute | solution.py:58
  373.7 3.9 collective-permute-start.7
  378.2 5.1 %collective-permute-start.16 = (bf16[40,384]{1,0:T(8,128)(2,1)S(1)}, bf16[40,384]{1,0:T(8,128)(2,1)S(1)}, u32[]{:S(2)}, u32[]{:S(2)}) collective-permute-start(bf16[40,384]{1,0:T(8,128)(2,1)S(1)} %bitcast.243), channel_id=1, source_target_pairs={{0,4},{1,5},{2,6},{3,7},{4,0},{5,1},{6,2},{7,3},{8,12},{9,13},{10,... | collective-permute-start | bytes 92168 | tf_op jit(solution)/shard_map/ppermute | solution.py:58
  381.6 3.1 collective-permute-start.17
  381.6 4.4 %collective-permute-start.15 = (bf16[40,384]{1,0:T(8,128)(2,1)S(1)}, bf16[40,384]{1,0:T(8,128)(2,1)S(1)}, u32[]{:S(2)}, u32[]{:S(2)}) collective-permute-start(bf16[40,384]{1,0:T(8,128)(2,1)S(1)} %bitcast.241), channel_id=1, source_target_pairs={{0,2},{1,3},{2,4},{3,5},{4,6},{5,7},{6,0},{7,1},{8,10},{9,11},{10,... | collective-permute-start | bytes 92168 | tf_op jit(solution)/shard_map/ppermute | solution.py:58
  386.3 14.8 %copy-start.26 = (bf16[591,768]{1,0:T(8,128)(2,1)S(1)}, bf16[591,768]{1,0:T(8,128)(2,1)}, u32[]{:S(2)}) copy-start(bf16[591,768]{1,0:T(8,128)(2,1)} %get-tuple-element.50) | copy-start | bytes 2723332
  386.3 16.1 %collective-permute-start.18 = (f32[24,384]{1,0:T(8,128)S(1)}, f32[24,384]{1,0:T(8,128)S(1)}, u32[]{:S(2)}, u32[]{:S(2)}) collective-permute-start(f32[24,384]{1,0:T(8,128)S(1)} %bitcast.239), channel_id=1, source_target_pairs={{0,1},{1,0},{2,3},{3,2},{4,5},{5,4},{6,7},{7,6},{8,9},{9,8},{10,11... | collective-permute-start | bytes 110600 | tf_op jit(solution)/shard_map/ppermute | solution.py:58
  410.7 4.8 %collective-permute-start.22 = (bf16[112,384]{1,0:T(8,128)(2,1)S(1)}, bf16[112,384]{1,0:T(8,128)(2,1)S(1)}, u32[]{:S(2)}, u32[]{:S(2)}) collective-permute-start(bf16[112,384]{1,0:T(8,128)(2,1)S(1)} %get-tuple-element.59), channel_id=1, source_target_pairs={{0,2},{1,3},{2,4},{3,5},{4,6},{5,7},{6,0},{7,1},{8,10},{9,11},{10,... | collective-permute-start | bytes 258056 | tf_op jit(solution)/shard_map/ppermute | solution.py:58
  412.0 3.5 collective-permute-start.24
  413.5 5.6 %collective-permute-start.23 = (bf16[112,384]{1,0:T(8,128)(2,1)S(1)}, bf16[112,384]{1,0:T(8,128)(2,1)S(1)}, u32[]{:S(2)}, u32[]{:S(2)}) collective-permute-start(bf16[112,384]{1,0:T(8,128)(2,1)S(1)} %get-tuple-element.61), channel_id=1, source_target_pairs={{0,4},{1,5},{2,6},{3,7},{4,0},{5,1},{6,2},{7,3},{8,12},{9,13},{10,... | collective-permute-start | bytes 258056 | tf_op jit(solution)/shard_map/ppermute | solution.py:58
  419.8 3.7 collective-permute-start.25
  (41 other events, 114.1 us)
Sparse Core Ops, SparseCore 0:
  19.1 82.0 all-gather.1
  326.4 81.4 reduce-scatter.1
